TPU v7x, 512 devices: a whole 4x4x16 slice. The times are simulated.
512 devices in a mesh: dp: 32 (over y_hi, z), tensor: 16 (over x, y_lo, core).
Axes of the slice: x: 4, y: 4 (y_hi: 2, y_lo: 2; y = y_hi * 2 + y_lo), z: 16, core: 2. Of those that a mesh axis runs over, the one named last changes fastest.
Arguments:
- cotangent: bfloat16 [4096, 4096], P('dp', 'tensor'), may hold values from -6 to 6
- gate_pre: bfloat16 [4096, 14336], P('dp', 'tensor'), may hold values from -6 to 6
- up_pre: bfloat16 [4096, 14336], P('dp', 'tensor'), may hold values from -6 to 6
- down_weight: bfloat16 [14336, 4096], P('tensor', 'dp'), may hold values from -0.046875 to 0.046875
Outputs:
- grad_gate: bfloat16 [4096, 14336], P('dp', 'tensor')
- grad_up: bfloat16 [4096, 14336], P('dp', 'tensor')
- grad_down: float32 [14336, 4096], P('tensor', 'dp')
All inputs are finite; a program needn't handle non-finite values.
Results may differ from a plain program's by a relative error of at most 0.003.
Values may be sent and summed in bfloat16 or wider, within the bound.
A program may use at most 64 MiB of HBM per device.

v0:
```python
import jax
import jax.numpy as jnp
from jax import lax
from jax.sharding import PartitionSpec as P


def shards(cotangent, gate_pre, up_pre, down_weight):
    gathered = lax.all_gather(cotangent, "tensor", axis=1, tiled=True)
    gate_vals = gate_pre.astype(jnp.float32)
    up_vals = up_pre.astype(jnp.float32)
    sigma = jax.nn.sigmoid(gate_vals)
    act_vals = gate_vals * sigma
    hidden = (act_vals * up_vals).astype(jnp.bfloat16)
    total_tokens = gathered.shape[0] * lax.axis_size("dp")
    dhid = lax.dot_general(
        gathered,
        lax.all_gather(down_weight, "dp", axis=1, tiled=True),
        (((1,), (1,)), ((), ())),
        preferred_element_type=jnp.float32,
    )
    feature_cols = lax.all_to_all(gathered, "dp", split_axis=1, concat_axis=0, tiled=True)
    summed = lax.dot_general(
        lax.all_gather(hidden, "dp", axis=0, tiled=True),
        feature_cols,
        (((0,), (0,)), ((), ())),
        preferred_element_type=jnp.float32,
    )
    grad_down = summed * total_tokens ** (-0.5)
    grad_up = (dhid * act_vals).astype(jnp.bfloat16)
    grad_gate = (dhid * up_vals * sigma * (1.0 + gate_vals * (1.0 - sigma))).astype(jnp.bfloat16)
    return (grad_gate, grad_up, grad_down)


def solution(mesh):
    in_specs = (P("dp", "tensor"), P("dp", "tensor"), P("dp", "tensor"), P("tensor", "dp"))
    out_specs = (P("dp", "tensor"), P("dp", "tensor"), P("tensor", "dp"))
    return jax.shard_map(shards, mesh=mesh, in_specs=in_specs, out_specs=out_specs, check_vma=False)
```

profile of v0, /device:TPU:6, one launch (start us, length us, event | category | flops | bytes accessed | tf_op | source)
XLA Modules:
  0.0 473.7 jit_solution(12646536183798980077)
XLA Ops:
  7.2 0.0 all-gather.4.cloned.1.call-start
  7.2 1.6 copy.7
  8.8 0.0 all-gather.4.cloned.1.call-update
  8.8 0.0 all-gather.6.cloned.1.call-start
  8.9 0.7 all-gather.6.cloned.1.call-update
  9.6 0.0 all-gather.8.cloned.1.call-start
  9.6 44.7 %all-gather.4.cloned.1.call-done = bf16[128,4096]{0,1:T(8,128)(2,1)} async-done(((bf16[128,256]{0,1:T(8,128)(2,1)}), bf16[128,4096]{0,1:T(8,128)(2,1)}) %all-gather.4.cloned.1.call-update) | async-done | bytes 1048592 | tf_op jit(solution)/shard_map/all_gather | solution.py:8
  54.3 0.0 copy-start
  54.3 203.2 %all-gather.6.cloned.1.call-done = bf16[896,4096]{1,0:T(8,128)(2,1)} async-done(((bf16[896,128]{1,0:T(8,128)(2,1)}), bf16[896,4096]{1,0:T(8,128)(2,1)}) %all-gather.6.cloned.1.call-update) | async-done | bytes 7340048 | tf_op jit(solution)/shard_map/all_gather | solution.py:17
  257.5 6.7 %multiply_convert_fusion = (bf16[128,896]{1,0:T(8,128)(2,1)}, bf16[128,896]{1,0:T(8,128)(2,1)}, bf16[128,896]{1,0:T(8,128)(2,1)}) fusion(bf16[128,896]{1,0:T(8,128)(2,1)} %param.5, bf16[128,896]{1,0:T(8,128)(2,1)} %param.6, bf16[128,4096]{0,1:T(8,128)(2,1)} %all-gather.4.cloned.1.call-done, bf16[896,4096]{1,0:T(8,128)(2,1)} %all-gather.6.cloned.1.call-done), kind=kOutput, calls=%fused_computation.14 | convolution fusion | flops 941473792 | bytes 9535488 | tf_op jit(solution)/shard_map/dot_general | solution.py:15
  264.2 0.0 all-gather.8.cloned.1.call-update
  264.2 0.0 copy-done
  264.3 62.4 %all_to_all.19 = bf16[128,32,128]{0,2,1:T(8,128)(2,1)S(1)} all-to-all(bf16[128,32,128]{0,2,1:T(8,128)(2,1)S(1)} %bitcast.8), channel_id=1, replica_groups=mesh['dp'=32,'tensor'=16] {'dp'}, dimensions={1} | all-to-all | bytes 2097152 | tf_op jit(solution)/shard_map/all_to_all | solution.py:21
  326.7 0.7 copy.8
  327.4 133.9 %all-gather.8.cloned.1.call-done = bf16[4096,896]{1,0:T(8,128)(2,1)} async-done(((bf16[128,896]{1,0:T(8,128)(2,1)}), bf16[4096,896]{1,0:T(8,128)(2,1)}) %all-gather.8.cloned.1.call-update) | async-done | bytes 7340048 | tf_op jit(solution)/shard_map/all_gather | solution.py:23
  461.2 5.9 %convolution_multiply_fusion = f32[896,128]{1,0:T(8,128)} fusion(bf16[4096,896]{1,0:T(8,128)(2,1)} %all-gather.8.cloned.1.call-done, bf16[4096,128]{1,0:T(8,128)(2,1)S(1)} %bitcast.9), kind=kOutput, calls=%fused_computation | convolution fusion | flops 939638784 | bytes 8847360 | tf_op jit(solution)/shard_map/dot_general | solution.py:22
Async XLA Ops:
  7.2 47.2 %all-gather.4.cloned.1.call-start = ((), (), s32[]{:S(2)}) async-start(), calls=%async_computation.1 | async-start | bytes 1114112 | tf_op jit(solution)/shard_map/all_gather | solution.py:8
  8.8 248.7 %all-gather.6.cloned.1.call-start = ((), (), s32[]{:S(2)}) async-start(), calls=%async_computation.2 | async-start | bytes 7569408 | tf_op jit(solution)/shard_map/all_gather | solution.py:17
  9.6 451.7 %all-gather.8.cloned.1.call-start = ((), (), s32[]{:S(2)}) async-start(), calls=%async_computation.3 | async-start | bytes 7569408 | tf_op jit(solution)/shard_map/all_gather | solution.py:23
  54.3 209.9 %copy-start = (bf16[128,4096]{0,1:T(8,128)(2,1)S(1)}, bf16[128,4096]{0,1:T(8,128)(2,1)}, u32[]{:S(2)}) copy-start(bf16[128,4096]{0,1:T(8,128)(2,1)} %all-gather.4.cloned.1.call-done) | copy-start | bytes 3145732
Sparse Core Ops, SparseCore 0:
  10.7 43.5 all-gather.3
  57.2 200.2 all-gather.5
  264.4 196.7 all-gather.7
where the time goes:
time: 474 us
  waiting for transfers between devices  382 us (81%)
  blocking collectives  62.4 us (13%)
  between operations  13.8 us (3%)
  matrix products  12.7 us (3%)
    all_gather x1, waiting for transfers between devices, shards(): lax.all_gather(down_weight, 'dp', axis=1, tiled=True)  203 us
    all_gather x1, waiting for transfers between devices, shards(): lax.all_gather(hidden, 'dp', axis=0, tiled=True)  134 us
    all_to_all x1, blocking collectives, shards(): lax.all_to_all(gathered, 'dp', split_axis=1, concat_axis=0, tiled=True)  62.4 us
    all_gather x1, waiting for transfers between devices, shards(): gathered = lax.all_gather(cotangent, 'tensor', axis=1, tiled=True)  44.7 us
  transfers between devices with their start and end apart: 3, of which 3 were waited for; matrix products, arithmetic and copies ran while one was open for 0% of the time, Pallas kernels for 0%

commit v1 on v0

v1 whole, which is shorter than its diff:
```python
import jax
import jax.numpy as jnp
from jax import lax
from jax.experimental import pallas as pl
from jax.experimental.pallas import tpu as pltpu
from jax.sharding import PartitionSpec as P

MESH = pl.DeviceIdType.MESH
F32, BF16 = jnp.float32, jnp.bfloat16
NX, NZ = 4, 16
NK = NZ // 2
B = 128
FD = 896
R = FD // NK
RS = NX * R
NC, CH = 4, 256

GRAD_SUM = BF16
GRAD_BACK = F32
DOWN_SUM = BF16
DOWN_BACK = BF16


def kernel(cot, gate, up, weight, o_gate, o_up, o_down,
           hid_t, f_up, f_gate, cot_b, w_g, h_g,
           d_f, d_p, d_r, d_s, d_own,
           g_f, g_p, g_r, g_s, g_own,
           sem_ring_r, sem_ring_l, sem_d, sem_g, sem):
    i, j = lax.axis_index("dp"), lax.axis_index("tensor")
    yh, z = i // NZ, i % NZ
    x, yl, c = j // 4, (j // 2) % 2, j % 2
    y = yh * 2 + yl
    par = (z + yl) % 2
    me = i * 16 + j

    def dev(x, yh, yl, z, c):
        return yh * NZ + z, x * 4 + yl * 2 + c

    def is_me(d):
        return d[0] * 16 + d[1] == me

    names = ["cot_send", "cot_recv", "w_send", "w_recv", "h_send", "h_recv", "ring_send_r", "ring_send_l",
             "sib_send", "sib_recv", "wg_send", "wg_recv", "hg_send", "hg_recv", "ds_send", "gs_send",
             "db_send", "db_recv", "gb_send", "gb_recv"]
    sems = {n: sem.at[k] for k, n in enumerate(names)}

    def remote(src, dst, send, recv, d):
        return pltpu.make_async_remote_copy(
            src_ref=src, dst_ref=dst, send_sem=send, recv_sem=recv, device_id=d, device_id_type=MESH)

    def send_any(src, dst, send, recv, d):
        @pl.when(is_me(d))
        def _():
            pltpu.make_async_copy(src, dst, recv).start()

        @pl.when(jnp.logical_not(is_me(d)))
        def _():
            remote(src, dst, send, recv, d).start()

    def wait(ref, s):
        pltpu.make_async_copy(ref, ref, s).wait()

    h_dst = [dev(x, yh, z % 2, 2 * s + c, yl) for s in range(NK)]
    w_dst = [dev(2 * yh + z % 2, x // 2, x % 2, 2 * s + c, yl) for s in range(NK)]
    c_dst = [dev(2 * (x // 2) + e, yh, z % 2, z, c) for e in range(2)]
    h_src = [dev(x, yh, c, 2 * k + yl, z % 2) for k in range(NK)]
    w_src = [dev(y, x // 2, c, 2 * k + x % 2, z % 2) for k in range(NK)]
    c_src = [dev(2 * (x // 2) + a, yh, b, z, c) for a in range(2) for b in range(2)]
    right, left = dev(x, yh, yl, (z + 1) % NZ, c), dev(x, yh, yl, (z + NZ - 1) % NZ, c)
    sibling = dev(x, yh, yl, z, 1 - c)
    x_dst = [dev((x + o) % 4, yh, yl, z, c) for o in range(1, 4)]
    y_idx = [(y + o) % 4 for o in range(1, 4)]
    y_dst = [dev(x, v // 2, v % 2, z, c) for v in y_idx]

    barrier = pltpu.get_barrier_semaphore()

    def greet(d):
        pl.semaphore_signal(barrier, inc=1, device_id=d, device_id_type=MESH)

    for d in h_src + w_src:
        @pl.when(jnp.logical_not(is_me(d)))
        def _():
            greet(d)
    for d in c_src:
        @pl.when(jnp.logical_and(par == 0, jnp.logical_not(is_me(d))))
        def _():
            greet(d)
    for d in [right, left, sibling] + x_dst + y_dst:
        greet(d)

    for b in range(FD // 128):
        cols = slice(b * 128, (b + 1) * 128)
        g, u = gate[:, cols].astype(F32), up[:, cols].astype(F32)
        sig = jax.nn.sigmoid(g)
        act = g * sig
        f_up[:, cols] = act
        f_gate[:, cols] = u * sig * (1.0 + g * (1.0 - sig))
        hid_t[cols, :] = (act * u).T.astype(BF16)

    def others(dsts):
        n = jnp.int32(0)
        for d in dsts:
            n = n + jnp.where(is_me(d), 0, 1)
        return n

    n_h, n_w, n_c = others(h_dst), others(w_dst), others(c_dst)
    pl.semaphore_wait(barrier, n_h + n_w + n_c + 9)

    for e in range(2):
        send_any(cot.at[:, pl.ds(e * B, B)],
                 cot_b.at[c * 2 + x % 2, pl.ds((z // 2) * B, B), pl.ds(yl * B, B)],
                 sems["cot_send"], sems["cot_recv"], c_dst[e])
    kz = z // 2
    for s in range(NK):
        send_any(weight.at[pl.ds(s * R, R)],
                 w_g.at[(kz % 2) * 2 + kz // 4, pl.ds(x * R, R), pl.ds(((kz // 2) % 2) * B, B)],
                 sems["w_send"], sems["w_recv"], w_dst[s])

    def send_hidden():
        for s in range(NK):
            send_any(hid_t.at[pl.ds(s * R, R)],
                     h_g.at[kz // 2, pl.ds(x * R, R), pl.ds((kz % 2) * B, B)],
                     sems["h_send"], sems["h_recv"], h_dst[s])

    def panel(zt):
        return cot_b.at[pl.ds(2 * c, 2), pl.ds(((zt + 2 * NZ) % NZ) // 2 * B, B)]

    def forward(ref, d, send, recv):
        remote(ref, ref, send, recv, d).start()

    for t in range(4):
        dist = 2 * t + par
        if t == 0:
            @pl.when(par == 0)
            def _():
                wait(panel(z), sems["cot_recv"])

            @pl.when(par == 1)
            def _():
                wait(panel(z - dist), sem_ring_r.at[0])
                wait(panel(z + dist), sem_ring_l.at[0])
        else:
            wait(panel(z - dist), sem_ring_r.at[t])
            wait(panel(z + dist), sem_ring_l.at[t])
        forward(panel(z - dist), right, sems["ring_send_r"], sem_ring_r.at[t + par])
        if t < 3:
            forward(panel(z + dist), left, sems["ring_send_l"], sem_ring_l.at[t + par])
        else:
            @pl.when(par == 0)
            def _():
                forward(panel(z + dist), left, sems["ring_send_l"], sem_ring_l.at[t])
        forward(panel(z - dist), sibling, sems["sib_send"], sems["sib_recv"])
        if t > 0:
            forward(panel(z + dist), sibling, sems["sib_send"], sems["sib_recv"])
        else:
            @pl.when(par == 1)
            def _():
                forward(panel(z + dist), sibling, sems["sib_send"], sems["sib_recv"])
        if t == 0:
            send_hidden()

    @pl.when(par == 0)
    def _():
        wait(panel(z - 8), sem_ring_r.at[4])
        forward(panel(z - 8), sibling, sems["sib_send"], sems["sib_recv"])

    mine_w = w_g.at[:, pl.ds(y * R, R)]
    mine_h = h_g.at[:, pl.ds(x * R, R)]
    three = h_g.at[:, pl.ds(0, 3 * R)]
    wait(mine_w, sems["w_recv"])
    for d in y_dst:
        forward(mine_w, d, sems["wg_send"], sems["wg_recv"])
    wait(mine_h, sems["h_recv"])
    for d in x_dst:
        forward(mine_h, d, sems["hg_send"], sems["hg_recv"])

    wait(cot_b.at[pl.ds(2 * (1 - c), 2)], sems["sib_recv"])
    wait(three, sems["wg_recv"])

    @pl.loop(0, NC)
    def _(n):
        rows = pl.ds(pl.multiple_of(n * CH, CH), CH)
        total = jnp.zeros((RS, CH), F32)
        for q in range(NC):
            total += lax.dot_general(w_g[q], cot_b[q, rows, :], (((1,), (1,)), ((), ())),
                                     preferred_element_type=F32)
        d_f[n] = total
        for v in range(NX):
            d_p[v, n] = total[v * R:(v + 1) * R].astype(GRAD_SUM)
        for o in range(1, 4):
            remote(d_p.at[(x + o) % 4, n], d_r.at[o - 1, n], sems["ds_send"], sem_d.at[n], x_dst[o - 1]).start()

    wait(three, sems["hg_recv"])

    @pl.loop(0, NC)
    def _(n):
        total = jnp.zeros((RS, CH), F32)
        for q in range(NC):
            total += jnp.dot(h_g[q], cot_b[n, q * CH:(q + 1) * CH, :], preferred_element_type=F32)
        g_f[n] = total
        for v in range(NX):
            g_p[v, n] = total[v * R:(v + 1) * R].astype(DOWN_SUM)
        for o in range(1, 4):
            remote(g_p.at[y_idx[o - 1], n], g_r.at[o - 1, n], sems["gs_send"], sem_g.at[n], y_dst[o - 1]).start()

    back = pl.ds(pl.multiple_of((z // 2) * R, R), R)
    for n in range(NC):
        wait(d_r.at[:, n], sem_d.at[n])
        total = d_f[n, pl.ds(pl.multiple_of(x * R, R), R), :]
        for o in range(3):
            total += d_r[o, n].astype(F32)
        for a in range(2):
            k = 2 * n + a
            d_s[k] = total[:, a * B:(a + 1) * B].astype(GRAD_BACK)
            send_any(d_s.at[k], d_own.at[back], sems["db_send"], sems["db_recv"], h_src[k])
    for n in range(NC):
        wait(g_r.at[:, n], sem_g.at[n])
        total = g_f[n, pl.ds(pl.multiple_of(y * R, R), R), :]
        for o in range(3):
            total += g_r[o, n].astype(F32)
        for a in range(2):
            k = 4 * (n % 2) + 2 * a + n // 2
            g_s[k] = total[:, a * B:(a + 1) * B].astype(DOWN_BACK)
            send_any(g_s.at[k], g_own.at[back], sems["gb_send"], sems["gb_recv"], w_src[k])

    wait(d_own, sems["db_recv"])
    for b in range(FD // 128):
        cols = slice(b * 128, (b + 1) * 128)
        dhid = d_own[cols, :].astype(F32).T
        o_up[:, cols] = (dhid * f_up[:, cols]).astype(BF16)
        o_gate[:, cols] = (dhid * f_gate[:, cols]).astype(BF16)
    wait(g_own, sems["gb_recv"])
    scale = 1.0 / 64.0
    o_down[...] = g_own[...].astype(F32) * scale

    def wait_all(ref, s, count, most):
        for k in (most - 1, most):
            @pl.when(count == k)
            def _():
                wait(ref.at[pl.ds(0, k)], s)

    def wait_rows(ref, s, count):
        for k in (NK - 1, NK):
            @pl.when(count == k)
            def _():
                wait(ref.at[pl.ds(0, k * R)], s)

    for k in (1, 2):
        @pl.when(n_c == k)
        def _():
            wait(cot.at[:, pl.ds(0, k * B)], sems["cot_send"])
    wait_rows(weight, sems["w_send"], n_w)
    wait_rows(hid_t, sems["h_send"], n_h)
    wait(cot_b.at[pl.ds(0, 2), pl.ds(0, 4 * B)], sems["ring_send_r"])

    @pl.when(par == 0)
    def _():
        wait(cot_b.at[pl.ds(0, 2), pl.ds(0, 4 * B)], sems["ring_send_l"])

    @pl.when(par == 1)
    def _():
        wait(cot_b.at[pl.ds(0, 2), pl.ds(0, 3 * B)], sems["ring_send_l"])

    wait(cot_b.at[pl.ds(0, 2)], sems["sib_send"])
    wait(three, sems["wg_send"])
    wait(three, sems["hg_send"])
    wait(d_r, sems["ds_send"])
    wait(g_r, sems["gs_send"])
    wait_all(d_s, sems["db_send"], n_h, NK)
    wait_all(g_s, sems["gb_send"], n_w, NK)


def shards(cotangent, gate_pre, up_pre, down_weight):
    vmem = pl.BlockSpec(memory_space=pltpu.VMEM)
    dma = pltpu.SemaphoreType.DMA
    return pl.pallas_call(
        kernel,
        name="swiglu_down_backward",
        out_shape=(
            jax.ShapeDtypeStruct((B, FD), BF16),
            jax.ShapeDtypeStruct((B, FD), BF16),
            jax.ShapeDtypeStruct((FD, B), F32),
        ),
        in_specs=[vmem] * 4,
        out_specs=(vmem,) * 3,
        scratch_shapes=[
            pltpu.VMEM((FD, B), BF16),
            pltpu.VMEM((B, FD), F32),
            pltpu.VMEM((B, FD), F32),
            pltpu.VMEM((NC, NK * B, CH), BF16),
            pltpu.VMEM((NC, RS, CH), BF16),
            pltpu.VMEM((NC, RS, CH), BF16),
            pltpu.VMEM((NC, RS, CH), F32),
            pltpu.VMEM((NX, NC, R, CH), GRAD_SUM),
            pltpu.VMEM((3, NC, R, CH), GRAD_SUM),
            pltpu.VMEM((NK, R, B), GRAD_BACK),
            pltpu.VMEM((FD, B), GRAD_BACK),
            pltpu.VMEM((NC, RS, CH), F32),
            pltpu.VMEM((NX, NC, R, CH), DOWN_SUM),
            pltpu.VMEM((3, NC, R, CH), DOWN_SUM),
            pltpu.VMEM((NK, R, B), DOWN_BACK),
            pltpu.VMEM((FD, B), DOWN_BACK),
            dma((5,)), dma((4,)), dma((NC,)), dma((NC,)), dma((20,)),
        ],
        compiler_params=pltpu.CompilerParams(
            collective_id=0, has_side_effects=True, vmem_limit_bytes=48 * 2**20),
        cost_estimate=pl.CostEstimate(flops=4 * RS * 1024 * 1024, bytes_accessed=2 * 2**20, transcendentals=B * FD),
    )(cotangent, gate_pre, up_pre, down_weight)


def solution(mesh):
    in_specs = (P("dp", "tensor"), P("dp", "tensor"), P("dp", "tensor"), P("tensor", "dp"))
    out_specs = (P("dp", "tensor"), P("dp", "tensor"), P("tensor", "dp"))
    return jax.shard_map(shards, mesh=mesh, in_specs=in_specs, out_specs=out_specs, check_vma=False)
```

time: 474 us -> 127 us (0.27)
  the two profiles are of different devices: /device:TPU:6 before, /device:TPU:1 now
where the time goes in v1:
time: 127 us
  Pallas kernels  121 us (95%)
  local copies, waits for them, and re-layouts  5.79 us (5%)
    pallas_call x1, Pallas kernels, shards(): pl.pallas_call(kernel, name='swiglu_down_backward', out_shape=(jax.ShapeD...  121 us
    unnamed x11, local copies, waits for them, and re-layouts  5.79 us

profile of v1, /device:TPU:1, one launch (start us, length us, event | category | flops | bytes accessed | tf_op | source)
XLA Modules:
  0.0 127.2 jit_solution(17009025635850805683)
XLA Ops:
  0.6 0.0 copy-start
  0.6 0.9 copy-done
  1.6 0.0 copy-start.1
  1.6 0.9 copy-done.1
  2.5 0.0 copy-start.2
  2.5 0.9 copy-done.2
  3.4 0.0 copy-start.3
  3.5 0.8 copy-done.3
  4.3 120.7 %swiglu_down_backward.1 = (bf16[128,896]{1,0:T(8,128)(2,1)S(1)}, bf16[128,896]{1,0:T(8,128)(2,1)S(1)}, f32[896,128]{1,0:T(8,128)S(1)}) custom-call(bf16[128,256]{1,0:T(8,128)(2,1)S(1)} %copy-done.3, bf16[128,896]{1,0:T(8,128)(2,1)S(1)} %copy-done, bf16[128,896]{1,0:T(8,128)(2,1)S(1)} %copy-done.1, bf16[896,128]{1,0:T(8,128)(2,1)S(1)} %copy-done.2), custom_call_target="tpu_custom_call" | custom-call | flops 1879048192 | bytes 2097152 | tf_op jit(solution)/shard_map/swiglu_down_backward/pallas_call | solution.py:276
  125.0 0.7 copy.10
  125.7 0.7 copy.11
  126.4 0.8 copy.12
Async XLA Ops:
  0.6 0.9 copy-start
  1.6 0.9 copy-start.1
  2.5 0.9 copy-start.2
  3.4 0.8 copy-start.3

commit v2 on v1

v2 whole, which is shorter than its diff:
```python
import jax
import jax.numpy as jnp
from jax import lax
from jax.experimental import pallas as pl
from jax.experimental.pallas import tpu as pltpu
from jax.sharding import PartitionSpec as P

MESH = pl.DeviceIdType.MESH
F32, BF16 = jnp.float32, jnp.bfloat16
NX, NZ = 4, 16
NK = NZ // 2
B = 128
FD = 896
R = FD // NK
RS = NX * R
NC, CH = 4, 256

NP, PR = 2, B // 2
W_AT, H_AT = 1, 2

AHEAD = 2
W_FIRST = False
PASS_AT = 3

GRAD_SUM = BF16
GRAD_BACK = F32
DOWN_SUM = BF16
DOWN_BACK = BF16


def kernel(cot_in, gate_in, up_in, weight_in, o_gate, o_up, o_down,
           cot, gate, up, weight, hid_t, f_up, f_gate, cot_b, w_g, h_g,
           d_f, d_p, d_r, d_s, d_own,
           g_f, g_p, g_r, g_s, g_own,
           sem_near, sem_ring_r, sem_ring_l, sem_w, sem_h, sem_d, sem_g, sem_in, sem):
    i, j = lax.axis_index("dp"), lax.axis_index("tensor")
    yh, z = i // NZ, i % NZ
    x, yl, c = j // 4, (j // 2) % 2, j % 2
    y = yh * 2 + yl
    par = (z + yl) % 2
    me = i * 16 + j

    def dev(x, yh, yl, z, c):
        return yh * NZ + z, x * 4 + yl * 2 + c

    def is_me(d):
        return d[0] * 16 + d[1] == me

    names = ["cot_send", "w_send", "h_send", "ring_send_r", "ring_send_l",
             "sib_send", "sib_recv", "wg_send", "wg_recv", "hg_send", "hg_recv", "ds_send", "gs_send",
             "db_send", "db_recv", "gb_send", "gb_recv"]
    sems = {n: sem.at[k] for k, n in enumerate(names)}

    def remote(src, dst, send, recv, d):
        return pltpu.make_async_remote_copy(
            src_ref=src, dst_ref=dst, send_sem=send, recv_sem=recv, device_id=d, device_id_type=MESH)

    def send_any(src, dst, send, recv, d):
        @pl.when(is_me(d))
        def _():
            pltpu.make_async_copy(src, dst, recv).start()

        @pl.when(jnp.logical_not(is_me(d)))
        def _():
            remote(src, dst, send, recv, d).start()

    def wait(ref, s):
        pltpu.make_async_copy(ref, ref, s).wait()

    h_dst = [dev(x, yh, z % 2, 2 * s + c, yl) for s in range(NK)]
    w_dst = [dev(2 * yh + z % 2, x // 2, x % 2, 2 * s + c, yl) for s in range(NK)]
    near = (0, 1, -1, 2, -2)
    c_dst = [(o, e, dev(2 * (x // 2) + e, yh, z % 2, (z + o + NZ) % NZ, c)) for o in near for e in range(2)]
    h_src = [dev(x, yh, c, 2 * k + yl, z % 2) for k in range(NK)]
    w_src = [dev(y, x // 2, c, 2 * k + x % 2, z % 2) for k in range(NK)]
    c_src = [(abs(o) % 2, dev(2 * (x // 2) + a, yh, b, (z + o + NZ) % NZ, c))
             for o in near for a in range(2) for b in range(2)]
    right, left = dev(x, yh, yl, (z + 1) % NZ, c), dev(x, yh, yl, (z + NZ - 1) % NZ, c)
    right2, left2 = dev(x, yh, yl, (z + 2) % NZ, c), dev(x, yh, yl, (z + NZ - 2) % NZ, c)
    sibling = dev(x, yh, yl, z, 1 - c)
    x_dst = [dev((x + o) % 4, yh, yl, z, c) for o in range(1, 4)]
    y_idx = [(y + o) % 4 for o in range(1, 4)]
    y_dst = [dev(x, v // 2, v % 2, z, c) for v in y_idx]

    loads = [pltpu.make_async_copy(a, b, sem_in.at[k])
             for k, (a, b) in enumerate([(gate_in, gate), (up_in, up), (cot_in, cot), (weight_in, weight)])]
    for load in loads:
        load.start()

    barrier = pltpu.get_barrier_semaphore()

    def greet(d):
        pl.semaphore_signal(barrier, inc=1, device_id=d, device_id_type=MESH)

    for d in h_src + w_src:
        @pl.when(jnp.logical_not(is_me(d)))
        def _():
            greet(d)
    for odd, d in c_src:
        @pl.when(jnp.logical_and(par == odd, jnp.logical_not(is_me(d))))
        def _():
            greet(d)
    for d in [right, left, right2, left2, sibling] + x_dst + y_dst:
        greet(d)

    loads[0].wait()
    loads[1].wait()
    for b in range(FD // 128):
        cols = slice(b * 128, (b + 1) * 128)
        g, u = gate[:, cols].astype(F32), up[:, cols].astype(F32)
        sig = jax.nn.sigmoid(g)
        act = g * sig
        hid_t[cols, :] = (act * u).T.astype(BF16)

    def others(dsts):
        n = jnp.int32(0)
        for d in dsts:
            n = n + jnp.where(is_me(d), 0, 1)
        return n

    loads[2].wait()
    loads[3].wait()
    n_h, n_w, n_c = others(h_dst), others(w_dst), others([d for _, _, d in c_dst])
    pl.semaphore_wait(barrier, n_h + n_w + n_c + 11)

    kz = z // 2

    def send_cot():
        for o, e, d in c_dst:
            send_any(cot.at[:, pl.ds(e * B, B)],
                     cot_b.at[c * 2 + x % 2, pl.ds((z // 2) * B, B), pl.ds(yl * B, B)],
                     sems["cot_send"], sem_near.at[o + 2], d)

    def send_weights():
        for s in range(NK):
            send_any(weight.at[pl.ds(s * R, R)],
                     w_g.at[(kz % 2) * 2 + kz // 4, pl.ds(x * R, R), pl.ds(((kz // 2) % 2) * B, B)],
                     sems["w_send"], sem_w.at[kz], w_dst[s])

    if W_FIRST:
        send_weights()
        send_cot()
    else:
        send_cot()
        send_weights()

    def send_hidden():
        for s in range(NK):
            send_any(hid_t.at[pl.ds(s * R, R)],
                     h_g.at[kz // 2, pl.ds(x * R, R), pl.ds((kz % 2) * B, B)],
                     sems["h_send"], sem_h.at[kz], h_dst[s])

    for b in range(FD // 128):
        cols = slice(b * 128, (b + 1) * 128)
        g, u = gate[:, cols].astype(F32), up[:, cols].astype(F32)
        sig = jax.nn.sigmoid(g)
        f_up[:, cols] = g * sig
        f_gate[:, cols] = u * sig * (1.0 + g * (1.0 - sig))

    def panel(zt):
        return cot_b.at[pl.ds(2 * c, 2), pl.ds(((zt + 2 * NZ) % NZ) // 2 * B, B)]

    def forward(ref, d, send, recv):
        remote(ref, ref, send, recv, d).start()

    def piece(zt, q):
        return cot_b.at[pl.ds(2 * c, 2), pl.ds(((zt + 2 * NZ) % NZ) // 2 * B + q * PR, PR)]

    three = h_g.at[:, pl.ds(0, 3 * R)]

    def pass_weights():
        for q in range(NC):
            mine = w_g.at[q, pl.ds(y * R, R)]
            for a in range(2):
                wait(mine.at[:, pl.ds(a * B, B)], sem_w.at[(q % 2) * 4 + 2 * a + q // 2])
            for d in y_dst:
                forward(mine, d, sems["wg_send"], sems["wg_recv"])

    def pass_hidden():
        for q in range(NC):
            mine = h_g.at[q, pl.ds(x * R, R)]
            for a in range(2):
                wait(mine.at[:, pl.ds(a * B, B)], sem_h.at[2 * q + a])
            for d in x_dst:
                forward(mine, d, sems["hg_send"], sems["hg_recv"])

    def to_sibling(zt):
        forward(panel(zt), sibling, sems["sib_send"], sems["sib_recv"])

    def hand_on(zt, d, q, one, two, send, recv):
        forward(piece(zt, q), two, send, recv.at[(d + 2) * NP + q]) if two is not None else None
        forward(piece(zt, q), one, send, recv.at[(d + 1) * NP + q])

    for t in range(4):
        @pl.when(par == 0)
        def _():
            d = 2 * t + 2
            if t == 0:
                wait(panel(z - 2), sem_near.at[4])
                wait(panel(z + 2), sem_near.at[0])
            for q in range(NP):
                if t > 0:
                    wait(piece(z - d, q), sem_ring_r.at[d * NP + q])
                if t < 3:
                    hand_on(z - d, d, q, right, right2, sems["ring_send_r"], sem_ring_r)
                    if t > 0:
                        wait(piece(z + d, q), sem_ring_l.at[d * NP + q])
                    hand_on(z + d, d, q, left, left2 if t < 2 else None, sems["ring_send_l"], sem_ring_l)
            to_sibling(z - d)
            if t < 3:
                to_sibling(z + d)
            if t == 0:
                wait(panel(z), sem_near.at[2])
                to_sibling(z)

        @pl.when(par == 1)
        def _():
            d = 2 * t + 1
            if t == 0:
                wait(panel(z - 1), sem_near.at[3])
                wait(panel(z + 1), sem_near.at[1])
            else:
                for q in range(NP):
                    wait(piece(z - d, q), sem_ring_r.at[d * NP + q])
                    wait(piece(z + d, q), sem_ring_l.at[d * NP + q])
            to_sibling(z - d)
            to_sibling(z + d)

        if t == H_AT:
            send_hidden()
        if t == W_AT:
            pass_weights()

    wait(cot_b.at[pl.ds(2 * (1 - c), 2)], sems["sib_recv"])
    wait(three, sems["wg_recv"])

    def multiply_dhid(n):
        total = jnp.zeros((RS, CH), F32)
        for q in range(NC):
            total += lax.dot_general(w_g[q], cot_b[q, n * CH:(n + 1) * CH, :], (((1,), (1,)), ((), ())),
                                     preferred_element_type=F32)
        d_f[n] = total
        for v in range(NX):
            d_p[v, n] = total[v * R:(v + 1) * R].astype(GRAD_SUM)
        for o in range(1, 4):
            remote(d_p.at[(x + o) % 4, n], d_r.at[o - 1, n], sems["ds_send"], sem_d.at[n], x_dst[o - 1]).start()

    def multiply_down(n):
        total = jnp.zeros((RS, CH), F32)
        for q in range(NC):
            total += jnp.dot(h_g[q], cot_b[n, q * CH:(q + 1) * CH, :], preferred_element_type=F32)
        g_f[n] = total
        for v in range(NX):
            g_p[v, n] = total[v * R:(v + 1) * R].astype(DOWN_SUM)
        for o in range(1, 4):
            remote(g_p.at[y_idx[o - 1], n], g_r.at[o - 1, n], sems["gs_send"], sem_g.at[n], y_dst[o - 1]).start()

    back = pl.ds(pl.multiple_of((z // 2) * R, R), R)

    def reduce_dhid(n):
        wait(d_r.at[:, n], sem_d.at[n])
        total = d_f[n, pl.ds(pl.multiple_of(x * R, R), R), :]
        for o in range(3):
            total += d_r[o, n].astype(F32)
        for a in range(2):
            k = 2 * n + a
            d_s[k] = total[:, a * B:(a + 1) * B].astype(GRAD_BACK)
            send_any(d_s.at[k], d_own.at[back], sems["db_send"], sems["db_recv"], h_src[k])

    def reduce_down(n):
        wait(g_r.at[:, n], sem_g.at[n])
        total = g_f[n, pl.ds(pl.multiple_of(y * R, R), R), :]
        for o in range(3):
            total += g_r[o, n].astype(F32)
        for a in range(2):
            k = 4 * (n % 2) + 2 * a + n // 2
            g_s[k] = total[:, a * B:(a + 1) * B].astype(DOWN_BACK)
            send_any(g_s.at[k], g_own.at[back], sems["gb_send"], sems["gb_recv"], w_src[k])

    for n in range(NC + AHEAD):
        if n < NC:
            multiply_dhid(n)
        if n == PASS_AT:
            pass_hidden()
        if n >= AHEAD:
            reduce_dhid(n - AHEAD)
    wait(three, sems["hg_recv"])
    for n in range(NC + AHEAD):
        if n < NC:
            multiply_down(n)
        if n >= AHEAD:
            reduce_down(n - AHEAD)

    wait(d_own, sems["db_recv"])
    for b in range(FD // 128):
        cols = slice(b * 128, (b + 1) * 128)
        dhid = d_own[cols, :].astype(F32).T
        o_up[:, cols] = (dhid * f_up[:, cols]).astype(BF16)
        o_gate[:, cols] = (dhid * f_gate[:, cols]).astype(BF16)
    wait(g_own, sems["gb_recv"])
    scale = 1.0 / 64.0
    o_down[...] = g_own[...].astype(F32) * scale

    def wait_all(ref, s, count, most):
        for k in (most - 1, most):
            @pl.when(count == k)
            def _():
                wait(ref.at[pl.ds(0, k)], s)

    def wait_rows(ref, s, count):
        for k in (NK - 1, NK):
            @pl.when(count == k)
            def _():
                wait(ref.at[pl.ds(0, k * R)], s)

    for k in (0, 1):
        @pl.when(n_c == len(c_dst) - k)
        def _():
            wait(cot_b.at[0, pl.ds(0, (len(c_dst) - k) // 2 * B)], sems["cot_send"])
            if k:
                wait(cot.at[:, pl.ds(0, B)], sems["cot_send"])
    wait_rows(weight, sems["w_send"], n_w)
    wait_rows(hid_t, sems["h_send"], n_h)

    @pl.when(par == 0)
    def _():
        wait(cot_b.at[pl.ds(0, 2), pl.ds(0, 6 * B)], sems["ring_send_r"])
        wait(cot_b.at[pl.ds(0, 2), pl.ds(0, 5 * B)], sems["ring_send_l"])

    wait(cot_b.at[pl.ds(0, 2)], sems["sib_send"])
    wait(three, sems["wg_send"])
    wait(three, sems["hg_send"])
    wait(d_r, sems["ds_send"])
    wait(g_r, sems["gs_send"])
    wait_all(d_s, sems["db_send"], n_h, NK)
    wait_all(g_s, sems["gb_send"], n_w, NK)


def shards(cotangent, gate_pre, up_pre, down_weight):
    vmem = pl.BlockSpec(memory_space=pltpu.VMEM)
    dma = pltpu.SemaphoreType.DMA
    return pl.pallas_call(
        kernel,
        name="swiglu_down_backward",
        out_shape=(
            jax.ShapeDtypeStruct((B, FD), BF16),
            jax.ShapeDtypeStruct((B, FD), BF16),
            jax.ShapeDtypeStruct((FD, B), F32),
        ),
        in_specs=[pl.BlockSpec(memory_space=pltpu.HBM)] * 4,
        out_specs=(vmem,) * 3,
        scratch_shapes=[
            pltpu.VMEM((B, 2 * B), BF16),
            pltpu.VMEM((B, FD), BF16),
            pltpu.VMEM((B, FD), BF16),
            pltpu.VMEM((FD, B), BF16),
            pltpu.VMEM((FD, B), BF16),
            pltpu.VMEM((B, FD), F32),
            pltpu.VMEM((B, FD), F32),
            pltpu.VMEM((NC, NK * B, CH), BF16),
            pltpu.VMEM((NC, RS, CH), BF16),
            pltpu.VMEM((NC, RS, CH), BF16),
            pltpu.VMEM((NC, RS, CH), F32),
            pltpu.VMEM((NX, NC, R, CH), GRAD_SUM),
            pltpu.VMEM((3, NC, R, CH), GRAD_SUM),
            pltpu.VMEM((NK, R, B), GRAD_BACK),
            pltpu.VMEM((FD, B), GRAD_BACK),
            pltpu.VMEM((NC, RS, CH), F32),
            pltpu.VMEM((NX, NC, R, CH), DOWN_SUM),
            pltpu.VMEM((3, NC, R, CH), DOWN_SUM),
            pltpu.VMEM((NK, R, B), DOWN_BACK),
            pltpu.VMEM((FD, B), DOWN_BACK),
            dma((5,)), dma((9 * NP,)), dma((8 * NP,)), dma((NK,)), dma((NK,)), dma((NC,)), dma((NC,)), dma((4,)), dma((17,)),
        ],
        compiler_params=pltpu.CompilerParams(
            collective_id=0, has_side_effects=True, vmem_limit_bytes=60 * 2**20),
        cost_estimate=pl.CostEstimate(flops=4 * RS * 1024 * 1024, bytes_accessed=2 * 2**20, transcendentals=B * FD),
    )(cotangent, gate_pre, up_pre, down_weight)


def solution(mesh):
    in_specs = (P("dp", "tensor"), P("dp", "tensor"), P("dp", "tensor"), P("tensor", "dp"))
    out_specs = (P("dp", "tensor"), P("dp", "tensor"), P("tensor", "dp"))
    return jax.shard_map(shards, mesh=mesh, in_specs=in_specs, out_specs=out_specs, check_vma=False)
```

time: 127 us -> 113 us (0.89)
  the two profiles are of different devices: /device:TPU:1 before, /device:TPU:68 now
where the time goes in v2:
time: 113 us; the launch traced here: 112 us
  Pallas kernels  109 us (96%)
  local copies, waits for them, and re-layouts  3.17 us (3%)
    pallas_call x1, Pallas kernels, shards(): pl.pallas_call(kernel, name='swiglu_down_backward', out_shape=(jax.ShapeD...  109 us
    unnamed x7, local copies, waits for them, and re-layouts  3.17 us

profile of v2, /device:TPU:68, one launch (start us, length us, event | category | flops | bytes accessed | tf_op | source)
XLA Modules:
  0.0 112.3 jit_solution(7410405588825995419)
XLA Ops:
  0.6 108.5 %swiglu_down_backward.1 = (bf16[128,896]{1,0:T(8,128)(2,1)}, bf16[128,896]{1,0:T(8,128)(2,1)}, f32[896,128]{1,0:T(8,128)}) custom-call(bf16[128,256]{1,0:T(8,128)(2,1)} %cot_in.1, bf16[128,896]{1,0:T(8,128)(2,1)} %gate_in.1, bf16[128,896]{1,0:T(8,128)(2,1)} %up_in.1, bf16[896,128]{1,0:T(8,128)(2,1)} %weight_in.1), custom_call_target="tpu_custom_call" | custom-call | flops 1879048192 | bytes 2097152 | tf_op jit(solution)/shard_map/swiglu_down_backward/pallas_call | solution.py:342
  109.1 0.0 copy-start.1
  109.2 0.0 copy-start
  109.2 1.7 %copy.10 = bf16[128,896]{1,0:T(8,128)(2,1)} copy(bf16[128,896]{1,0:T(8,128)(2,1)} %get-tuple-element.6) | data formatting | bytes 458752
  110.9 0.0 copy-done.1
  110.9 0.7 copy.11
  111.6 0.0 copy-done
  111.6 0.8 copy.12
Async XLA Ops:
  109.1 1.7 %copy-start.1 = (bf16[128,896]{1,0:T(8,128)(2,1)S(1)}, bf16[128,896]{1,0:T(8,128)(2,1)}, u32[]{:S(2)}) copy-start(bf16[128,896]{1,0:T(8,128)(2,1)} %get-tuple-element.7) | copy-start | bytes 688132
  109.2 2.4 %copy-start = (f32[896,128]{1,0:T(8,128)S(1)}, f32[896,128]{1,0:T(8,128)}, u32[]{:S(2)}) copy-start(f32[896,128]{1,0:T(8,128)} %get-tuple-element.8) | copy-start | bytes 1376260

commit v3 on v2

--- a/solution.py
+++ b/solution.py
@@ -16,11 +16,10 @@
 NC, CH = 4, 256
 
 NP, PR = 2, B // 2
-W_AT, H_AT = 1, 2
 
 AHEAD = 2
-W_FIRST = False
-PASS_AT = 3
+ALL = range(NK)
+PLAN = ([("w", ALL), ("h", ALL)], [], ["pass_w", "pass_h"], [], [])
 
 GRAD_SUM = BF16
 GRAD_BACK = F32
@@ -131,21 +130,16 @@
                      cot_b.at[c * 2 + x % 2, pl.ds((z // 2) * B, B), pl.ds(yl * B, B)],
                      sems["cot_send"], sem_near.at[o + 2], d)
 
-    def send_weights():
-        for s in range(NK):
+    def send_weights(part):
+        for s in part:
             send_any(weight.at[pl.ds(s * R, R)],
                      w_g.at[(kz % 2) * 2 + kz // 4, pl.ds(x * R, R), pl.ds(((kz // 2) % 2) * B, B)],
                      sems["w_send"], sem_w.at[kz], w_dst[s])
 
-    if W_FIRST:
-        send_weights()
-        send_cot()
-    else:
-        send_cot()
-        send_weights()
-
-    def send_hidden():
-        for s in range(NK):
+    send_cot()
+
+    def send_hidden(part):
+        for s in part:
             send_any(hid_t.at[pl.ds(s * R, R)],
                      h_g.at[kz // 2, pl.ds(x * R, R), pl.ds((kz % 2) * B, B)],
                      sems["h_send"], sem_h.at[kz], h_dst[s])
@@ -186,6 +180,17 @@
 
     def to_sibling(zt):
         forward(panel(zt), sibling, sems["sib_send"], sems["sib_recv"])
+
+    def act(point):
+        for what in PLAN[point]:
+            if what == "pass_w":
+                pass_weights()
+            elif what == "pass_h":
+                pass_hidden()
+            else:
+                (send_weights if what[0] == "w" else send_hidden)(what[1])
+
+    act(0)
 
     def hand_on(zt, d, q, one, two, send, recv):
         forward(piece(zt, q), two, send, recv.at[(d + 2) * NP + q]) if two is not None else None
@@ -226,10 +231,7 @@
             to_sibling(z - d)
             to_sibling(z + d)
 
-        if t == H_AT:
-            send_hidden()
-        if t == W_AT:
-            pass_weights()
+        act(t + 1)
 
     wait(cot_b.at[pl.ds(2 * (1 - c), 2)], sems["sib_recv"])
     wait(three, sems["wg_recv"])
@@ -277,18 +279,13 @@
             g_s[k] = total[:, a * B:(a + 1) * B].astype(DOWN_BACK)
             send_any(g_s.at[k], g_own.at[back], sems["gb_send"], sems["gb_recv"], w_src[k])
 
+    wait(three, sems["hg_recv"])
     for n in range(NC + AHEAD):
         if n < NC:
             multiply_dhid(n)
-        if n == PASS_AT:
-            pass_hidden()
+            multiply_down(n)
         if n >= AHEAD:
             reduce_dhid(n - AHEAD)
-    wait(three, sems["hg_recv"])
-    for n in range(NC + AHEAD):
-        if n < NC:
-            multiply_down(n)
-        if n >= AHEAD:
             reduce_down(n - AHEAD)
 
     wait(d_own, sems["db_recv"])

time: 113 us -> 111 us (0.982)
  the two profiles are of different devices: /device:TPU:68 before, /device:TPU:10 now
where the time goes in v3:
time: 111 us
  Pallas kernels  107 us (96%)
  local copies, waits for them, and re-layouts  3.17 us (3%)
    pallas_call x1, Pallas kernels, shards(): pl.pallas_call(kernel, name='swiglu_down_backward', out_shape=(jax.ShapeD...  107 us
    unnamed x7, local copies, waits for them, and re-layouts  3.17 us

profile of v3, /device:TPU:10, one launch (start us, length us, event | category | flops | bytes accessed | tf_op | source)
XLA Modules:
  0.0 111.3 jit_solution(16682757407091563965)
XLA Ops:
  0.6 107.5 %swiglu_down_backward.1 = (bf16[128,896]{1,0:T(8,128)(2,1)}, bf16[128,896]{1,0:T(8,128)(2,1)}, f32[896,128]{1,0:T(8,128)}) custom-call(bf16[128,256]{1,0:T(8,128)(2,1)} %cot_in.1, bf16[128,896]{1,0:T(8,128)(2,1)} %gate_in.1, bf16[128,896]{1,0:T(8,128)(2,1)} %up_in.1, bf16[896,128]{1,0:T(8,128)(2,1)} %weight_in.1), custom_call_target="tpu_custom_call" | custom-call | flops 1879048192 | bytes 2097152 | tf_op jit(solution)/shard_map/swiglu_down_backward/pallas_call | solution.py:339
  108.1 0.0 copy-start.1
  108.1 0.0 copy-start
  108.1 1.7 %copy.10 = bf16[128,896]{1,0:T(8,128)(2,1)} copy(bf16[128,896]{1,0:T(8,128)(2,1)} %get-tuple-element.6) | data formatting | bytes 458752
  109.9 0.0 copy-done.1
  109.9 0.7 copy.11
  110.5 0.0 copy-done
  110.6 0.8 copy.12
Async XLA Ops:
  108.1 1.7 %copy-start.1 = (bf16[128,896]{1,0:T(8,128)(2,1)S(1)}, bf16[128,896]{1,0:T(8,128)(2,1)}, u32[]{:S(2)}) copy-start(bf16[128,896]{1,0:T(8,128)(2,1)} %get-tuple-element.7) | copy-start | bytes 688132
  108.1 2.4 %copy-start = (f32[896,128]{1,0:T(8,128)S(1)}, f32[896,128]{1,0:T(8,128)}, u32[]{:S(2)}) copy-start(f32[896,128]{1,0:T(8,128)} %get-tuple-element.8) | copy-start | bytes 1376260

commit v4 on v3

--- a/solution.py
+++ b/solution.py
@@ -19,7 +19,7 @@
 
 AHEAD = 2
 ALL = range(NK)
-PLAN = ([("w", ALL), ("h", ALL)], [], ["pass_w", "pass_h"], [], [])
+PLAN = ([("w", ALL), ("h", ALL)], ["pass_w"], ["pass_h"], [], [])
 
 GRAD_SUM = BF16
 GRAD_BACK = F32

time: 111 us -> 111 us (level)
  no operation moved by 1% of the time
where the time goes in v4:
time: 111 us
  Pallas kernels  107 us (96%)
  local copies, waits for them, and re-layouts  3.17 us (3%)
    pallas_call x1, Pallas kernels, shards(): pl.pallas_call(kernel, name='swiglu_down_backward', out_shape=(jax.ShapeD...  107 us
    unnamed x7, local copies, waits for them, and re-layouts  3.17 us

profile of v4, /device:TPU:10, one launch (start us, length us, event | category | flops | bytes accessed | tf_op | source)
XLA Modules:
  0.0 111.0 jit_solution(4024961283611145787)
XLA Ops:
  0.6 107.2 %swiglu_down_backward.1 = (bf16[128,896]{1,0:T(8,128)(2,1)}, bf16[128,896]{1,0:T(8,128)(2,1)}, f32[896,128]{1,0:T(8,128)}) custom-call(bf16[128,256]{1,0:T(8,128)(2,1)} %cot_in.1, bf16[128,896]{1,0:T(8,128)(2,1)} %gate_in.1, bf16[128,896]{1,0:T(8,128)(2,1)} %up_in.1, bf16[896,128]{1,0:T(8,128)(2,1)} %weight_in.1), custom_call_target="tpu_custom_call" | custom-call | flops 1879048192 | bytes 2097152 | tf_op jit(solution)/shard_map/swiglu_down_backward/pallas_call | solution.py:339
  107.8 0.0 copy-start.1
  107.8 0.0 copy-start
  107.8 1.7 %copy.10 = bf16[128,896]{1,0:T(8,128)(2,1)} copy(bf16[128,896]{1,0:T(8,128)(2,1)} %get-tuple-element.6) | data formatting | bytes 458752
  109.5 0.0 copy-done.1
  109.5 0.7 copy.11
  110.2 0.0 copy-done
  110.2 0.8 copy.12
Async XLA Ops:
  107.8 1.7 %copy-start.1 = (bf16[128,896]{1,0:T(8,128)(2,1)S(1)}, bf16[128,896]{1,0:T(8,128)(2,1)}, u32[]{:S(2)}) copy-start(bf16[128,896]{1,0:T(8,128)(2,1)} %get-tuple-element.7) | copy-start | bytes 688132
  107.8 2.4 %copy-start = (f32[896,128]{1,0:T(8,128)S(1)}, f32[896,128]{1,0:T(8,128)}, u32[]{:S(2)}) copy-start(f32[896,128]{1,0:T(8,128)} %get-tuple-element.8) | copy-start | bytes 1376260

commit v5 on v4

--- a/solution.py
+++ b/solution.py
@@ -19,7 +19,7 @@
 
 AHEAD = 2
 ALL = range(NK)
-PLAN = ([("w", ALL), ("h", ALL)], ["pass_w"], ["pass_h"], [], [])
+PLAN = ([("w", ALL), ("h", ALL)], ["pass_w", "pass_h"], [], [], [])
 
 GRAD_SUM = BF16
 GRAD_BACK = F32

time: 111 us -> 112 us (level)
  no operation moved by 1% of the time
where the time goes in v5:
time: 112 us; the launch traced here: 111 us
  Pallas kernels  108 us (96%)
  local copies, waits for them, and re-layouts  3.17 us (3%)
    pallas_call x1, Pallas kernels, shards(): pl.pallas_call(kernel, name='swiglu_down_backward', out_shape=(jax.ShapeD...  108 us
    unnamed x7, local copies, waits for them, and re-layouts  3.17 us

profile of v5, /device:TPU:10, one launch (start us, length us, event | category | flops | bytes accessed | tf_op | source)
XLA Modules:
  0.0 111.5 jit_solution(9292827828117005932)
XLA Ops:
  0.6 107.7 %swiglu_down_backward.1 = (bf16[128,896]{1,0:T(8,128)(2,1)}, bf16[128,896]{1,0:T(8,128)(2,1)}, f32[896,128]{1,0:T(8,128)}) custom-call(bf16[128,256]{1,0:T(8,128)(2,1)} %cot_in.1, bf16[128,896]{1,0:T(8,128)(2,1)} %gate_in.1, bf16[128,896]{1,0:T(8,128)(2,1)} %up_in.1, bf16[896,128]{1,0:T(8,128)(2,1)} %weight_in.1), custom_call_target="tpu_custom_call" | custom-call | flops 1879048192 | bytes 2097152 | tf_op jit(solution)/shard_map/swiglu_down_backward/pallas_call | solution.py:339
  108.3 0.0 copy-start.1
  108.3 0.0 copy-start
  108.3 1.7 %copy.10 = bf16[128,896]{1,0:T(8,128)(2,1)} copy(bf16[128,896]{1,0:T(8,128)(2,1)} %get-tuple-element.6) | data formatting | bytes 458752
  110.0 0.0 copy-done.1
  110.0 0.7 copy.11
  110.7 0.0 copy-done
  110.7 0.8 copy.12
Async XLA Ops:
  108.3 1.7 %copy-start.1 = (bf16[128,896]{1,0:T(8,128)(2,1)S(1)}, bf16[128,896]{1,0:T(8,128)(2,1)}, u32[]{:S(2)}) copy-start(bf16[128,896]{1,0:T(8,128)(2,1)} %get-tuple-element.7) | copy-start | bytes 688132
  108.3 2.4 %copy-start = (f32[896,128]{1,0:T(8,128)S(1)}, f32[896,128]{1,0:T(8,128)}, u32[]{:S(2)}) copy-start(f32[896,128]{1,0:T(8,128)} %get-tuple-element.8) | copy-start | bytes 1376260
